TPU v7x, 32 devices: a whole 2x2x4 slice. The times are simulated.
32 devices in a mesh: layer: 8 (over y, x, core), feat: 4 (over z).
Axes of the slice: x: 2, y: 2, z: 4, core: 2. Of those that a mesh axis runs over, the one named last changes fastest.
Arguments:
- pre_acts: bfloat16 [8, 512, 512], P('layer', None, 'feat'), may hold values from -6 to 6
- decoder: bfloat16 [8, 8, 512, 2048], P('layer', None, 'feat'), may hold values from -0.125 to 0.125
- dec_bias: bfloat16 [8, 2048], P('layer', 'feat'), may hold values from -3 to 3
- target: bfloat16 [8, 512, 2048], P('layer', None, 'feat'), may hold values from -6 to 6
Outputs:
- recon_error: float32 [8, 512, 2048], P('layer', None, 'feat')
- pre_grad: float32 [8, 512, 512], P('layer', None, 'feat')
All inputs are finite; a program needn't handle non-finite values.
Results may differ from a plain program's by a relative error of at most 0.015.
Values may be sent and summed in bfloat16 or wider, within the bound.
A program may use at most 64 MiB of HBM per device.

v0:
```python
import jax
import jax.numpy as jnp
from jax import lax
from jax.sharding import PartitionSpec as P


def on_device(pre_acts, decoder, dec_bias, target):
    my_layer = lax.axis_index("layer")
    token_count = pre_acts.shape[1]
    feat_width = pre_acts.shape[2]
    model_width = decoder.shape[3]
    shard_width = target.shape[2]
    activations = jnp.maximum(pre_acts, jnp.zeros((), pre_acts.dtype))
    pair_weights = decoder[0]
    piece = lax.all_gather(activations, "layer", axis=0, tiled=True)

    def add_one_source(offset, carried):
        weights = lax.dynamic_index_in_dim(pair_weights, offset, 0, keepdims=False)
        source_rows = lax.dynamic_index_in_dim(piece, offset, 0, keepdims=False)
        return lax.cond(
            offset <= my_layer,
            lambda value: value + jnp.dot(source_rows, weights, preferred_element_type=jnp.float32),
            lambda value: value,
            carried,
        )

    partial_value = lax.fori_loop(
        0, piece.shape[0], add_one_source, jnp.zeros((token_count, model_width), jnp.float32)
    )
    column_start = lax.axis_index("feat") * shard_width
    summed = lax.psum(partial_value.astype(jnp.bfloat16), "feat").astype(jnp.float32)
    full_target, full_bias = (
        lax.all_gather(target, "feat", axis=2, tiled=True),
        lax.all_gather(dec_bias, "feat", axis=1, tiled=True),
    )
    full_error = (
        summed + full_bias[0].astype(jnp.float32)[None, :] - full_target[0].astype(jnp.float32)
    )
    recon_error = lax.dynamic_slice_in_dim(full_error, column_start, shard_width, 1)[None]
    error_rounded = full_error.astype(jnp.bfloat16)

    def source_one_source(offset, carried):
        weights = lax.dynamic_index_in_dim(pair_weights, offset, 0, keepdims=False)
        value = lax.cond(
            offset <= my_layer,
            lambda rows: lax.dot_general(
                rows, weights, (((1,), (1,)), ((), ())), preferred_element_type=jnp.float32
            ),
            lambda rows: jnp.zeros((token_count, feat_width), jnp.float32),
            error_rounded,
        )
        return lax.dynamic_update_index_in_dim(carried, value, offset, 0)

    grad_sum = lax.psum_scatter(
        lax.fori_loop(
            0,
            1 * lax.axis_size("layer"),
            source_one_source,
            jnp.zeros((1 * lax.axis_size("layer"), token_count, feat_width), jnp.float32),
        ).astype(jnp.bfloat16),
        "layer",
        scatter_dimension=0,
        tiled=True,
    ).astype(jnp.float32)
    pre_grad = grad_sum * (pre_acts > 0).astype(jnp.float32)
    return (recon_error, pre_grad)


def solution(mesh):
    return jax.shard_map(
        on_device,
        mesh=mesh,
        in_specs=(
            P("layer", None, "feat"),
            P("layer", None, "feat", None),
            P("layer", "feat"),
            P("layer", None, "feat"),
        ),
        out_specs=(P("layer", None, "feat"), P("layer", None, "feat")),
        check_vma=False,
    )
```

profile of v0, /device:TPU:0, one launch (start us, length us, event | category | flops | bytes accessed | tf_op | source)
XLA Modules:
  0.0 241.4 jit_solution(8227289682518972324)
XLA Ops:
  7.2 0.0 all-gather.3.cloned.1.call-start
  7.2 1.6 broadcast_maximum_fusion
  8.8 0.0 all-gather.3.cloned.1.call-update
  8.8 0.0 all-gather.5.cloned.1.call-start
  8.9 0.7 all-gather.5.cloned.1.call-update
  9.6 0.0 all-reduce.2.cloned.1.call-start
  9.6 27.1 %all-gather.3.cloned.1.call-done = bf16[8,512,128]{2,1,0:T(8,128)(2,1)} async-done(((bf16[1,512,128]{2,1,0:T(8,128)(2,1)}), bf16[8,512,128]{2,1,0:T(8,128)(2,1)}) %all-gather.3.cloned.1.call-update) | async-done | bytes 1048592 | tf_op jit(solution)/shard_map/all_gather | solution.py:15
  36.7 2.5 %broadcast_in_dim.23 = f32[512,2048]{1,0:T(8,128)} broadcast(f32[]{:T(128)} %constant.85.clone.1), dimensions={} | broadcast | bytes 4194308 | tf_op jit(solution)/shard_map/broadcast_in_dim | solution.py:28
  39.2 5.1 %while.29 = (s32[]{:T(128)}, f32[512,2048]{1,0:T(8,128)}, s32[]{:T(128)}, bf16[8,512,128]{2,1,0:T(8,128)(2,1)}, bf16[8,128,2048]{2,1,0:T(8,128)(2,1)}, /*index=5*/s32[]{:T(128)}) while((s32[]{:T(128)}, f32[512,2048]{1,0:T(8,128)}, s32[]{:T(128)}, bf16[8,512,128]{2,1,0:T(8,128)(2,1)}, bf16[8,128,2048]{2,1,0:T(8,128)(2,1)}, ...), condition=%wide.region_3.4_spmd, body=%wide.region_0.3_spmd.sunk | while | flops 269484032 | bytes 9045115 | solution.py:27
  39.2 5.0 %conditional.4 = (f32[512,2048]{1,0:T(8,128)}) conditional(s32[]{:T(128)} %convert_element_type.52, f32[512,2048]{1,0:T(8,128)} %get-tuple-element.379, (bf16[8,512,128]{2,1,0:T(8,128)(2,1)}, s32[]{:T(128)}, bf16[8,128,2048]{2,1,0:T(8,128)(2,1)}, f32[512,2048]{1,0:T(8,128)}) %tuple.90), branch_computations={%region_1.1_spmd, %region_2.2_spmd} | conditional | flops 269484032 | bytes 9045000 | solution.py:20
  39.2 5.0 %convolution_add_fusion = f32[512,2048]{1,0:T(8,128)} fusion(f32[512,2048]{1,0:T(8,128)} %get-tuple-element.263, bf16[8,128,2048]{2,1,0:T(8,128)(2,1)} %get-tuple-element.266, s32[]{:T(128)} %get-tuple-element.265, bf16[8,512,128]{2,1,0:T(8,128)(2,1)} %get-tuple-element.264), kind=kOutput, calls=%fused_computation | convolution fusion | flops 269484032 | bytes 9044992 | tf_op jit(solution)/shard_map/while/body/eval_jaxpr/cond/branch_1_fun/dot_general | solution.py:22
  44.2 0.0 copy-start.1
  44.2 4.1 %convert_element_type.38 = bf16[512,2048]{1,0:T(8,128)(2,1)} convert(f32[512,2048]{1,0:T(8,128)} %get-tuple-element.286) | non-fusion elementwise | flops 1048576 | bytes 6291456 | tf_op jit(solution)/shard_map/convert_element_type | solution.py:31
  48.4 0.0 all-reduce.2.cloned.1.call-update
  48.4 0.0 reduce-scatter.2.cloned.1.call-start
  48.5 0.0 copy-done.1
  48.5 12.6 %all_gather.10 = bf16[1,2048]{1,0:T(2,128)(2,1)S(1)} all-gather(bf16[1,512]{1,0:T(2,128)(2,1)S(1)} %copy-done.1), channel_id=1, replica_groups=mesh['layer'=8,'feat'=4] {'feat'}, dimensions={1}, use_global_device_ids=true | all-gather | bytes 5120 | tf_op jit(solution)/shard_map/all_gather | solution.py:34
  61.1 23.2 %all-gather.5.cloned.1.call-done = bf16[1,512,2048]{2,1,0:T(8,128)(2,1)} async-done(((bf16[1,512,512]{2,1,0:T(8,128)(2,1)}), bf16[1,512,2048]{2,1,0:T(8,128)(2,1)}) %all-gather.5.cloned.1.call-update) | async-done | bytes 2097168 | tf_op jit(solution)/shard_map/all_gather | solution.py:33
  84.3 87.6 %all-reduce.2.cloned.1.call-done = bf16[512,2048]{1,0:T(8,128)(2,1)} async-done(((bf16[512,2048]{1,0:T(8,128)(2,1)}), bf16[512,2048]{1,0:T(8,128)(2,1)}) %all-reduce.2.cloned.1.call-update) | async-done | bytes 2097168 | tf_op jit(solution)/shard_map/psum | solution.py:31
  171.9 5.2 %fusion.8 = (bf16[512,2048]{1,0:T(8,128)(2,1)S(1)}, f32[512,2048]{1,0:T(8,128)}) fusion(bf16[1,512,2048]{2,1,0:T(8,128)(2,1)} %all-gather.5.cloned.1.call-done, f32[2048]{0:T(1024)S(1)} %bitcast.23, bf16[512,2048]{1,0:T(8,128)(2,1)} %all-reduce.2.cloned.1.call-done), kind=kLoop, calls=%fused_computation.15 | loop fusion | flops 5242880 | bytes 10493952 | tf_op jit(solution)/shard_map/convert_element_type | solution.py:40
  177.0 0.0 copy-start
  177.0 8.4 %while.30 = (s32[]{:T(128)}, bf16[8,512,128]{2,1,0:T(8,128)(2,1)}, s32[]{:T(128)}, bf16[8,128,2048]{2,1,0:T(8,128)(2,1)}, bf16[512,2048]{1,0:T(8,128)(2,1)S(1)}, /*index=5*/s32[]{:T(128)}) while((s32[]{:T(128)}, bf16[8,512,128]{2,1,0:T(8,128)(2,1)}, s32[]{:T(128)}, bf16[8,128,2048]{2,1,0:T(8,128)(2,1)}, bf16[512,2048]{1,0:T(8,128)(2,1)S(1)}, ...), condition=%wide.region_8.9_spmd, body=%wide.region_5.8_spmd.sunk | while | flops 268435456 | bytes 3277939 | solution.py:55
  177.0 1.9 conditional.5
  177.0 1.9 convolution_bitcast_fusion
  178.9 0.1 copy.11
  179.1 0.7 constant_dynamic-update-slice_fusion.2
  179.8 0.1 copy.11
  179.9 0.7 constant_dynamic-update-slice_fusion.2
  180.6 0.1 copy.11
  180.7 0.7 constant_dynamic-update-slice_fusion.2
  181.4 0.1 copy.11
  181.5 0.7 constant_dynamic-update-slice_fusion.2
  182.2 0.1 copy.11
  182.3 0.7 constant_dynamic-update-slice_fusion.2
  183.0 0.1 copy.11
  183.1 0.7 constant_dynamic-update-slice_fusion.2
  183.8 0.1 copy.11
  183.9 0.7 constant_dynamic-update-slice_fusion.2
  184.6 0.1 copy.11
  184.7 0.7 constant_dynamic-update-slice_fusion.2
  185.4 0.0 reduce-scatter.2.cloned.1.call-update
  185.4 2.3 dynamic-slice_bitcast_fusion
  187.7 45.6 %reduce-scatter.2.cloned.1.call-done = bf16[1,512,128]{2,1,0:T(8,128)(2,1)} async-done(((bf16[8,512,128]{2,1,0:T(8,128)(2,1)}), bf16[1,512,128]{2,1,0:T(8,128)(2,1)}) %reduce-scatter.2.cloned.1.call-update) | async-done | bytes 131088 | tf_op jit(solution)/shard_map/reduce_scatter | solution.py:54
  233.3 0.0 copy-done
  233.3 1.6 convert_select_fusion
  (23 shorter events, 0.2 us)
Async XLA Ops:
  7.2 29.5 %all-gather.3.cloned.1.call-start = ((), (), s32[]{:S(2)}) async-start(), calls=%async_computation.1 | async-start | bytes 1179648 | tf_op jit(solution)/shard_map/all_gather | solution.py:15
  8.8 75.5 %all-gather.5.cloned.1.call-start = ((), (), s32[]{:S(2)}) async-start(), calls=%async_computation.3 | async-start | bytes 2621440 | tf_op jit(solution)/shard_map/all_gather | solution.py:33
  9.6 162.3 %all-reduce.2.cloned.1.call-start = ((), (), s32[]{:S(2)}) async-start(), calls=%async_computation.2 | async-start | bytes 4194304 | tf_op jit(solution)/shard_map/psum | solution.py:31
  44.2 4.2 %copy-start.1 = (bf16[1,512]{1,0:T(2,128)(2,1)S(1)}, bf16[1,512]{1,0:T(2,128)(2,1)}, u32[]{:S(2)}) copy-start(bf16[1,512]{1,0:T(2,128)(2,1)} %param.14) | copy-start | bytes 3076
  48.4 184.9 %reduce-scatter.2.cloned.1.call-start = ((), (), s32[]{:S(2)}) async-start(), calls=%async_computation.4 | async-start | bytes 1179648 | tf_op jit(solution)/shard_map/reduce_scatter | solution.py:54
  177.0 56.3 %copy-start = (bf16[1,512,128]{2,1,0:T(8,128)(2,1)S(1)}, bf16[1,512,128]{2,1,0:T(8,128)(2,1)}, u32[]{:S(2)}) copy-start(bf16[1,512,128]{2,1,0:T(8,128)(2,1)} %param.12) | copy-start | bytes 393220
Sparse Core Ops, SparseCore 0:
  10.5 26.1 all-gather.2
  38.3 45.9 all-gather.4
  86.7 85.1 all-reduce.1
  185.6 47.6 reduce-scatter.1
where the time goes:
time: 242 us; the launch traced here: 241 us
  waiting for transfers between devices  184 us (76%)
  between operations  13.8 us (6%)
  blocking collectives  12.6 us (5%)
  other arithmetic  12.5 us (5%)
  local copies, waits for them, and re-layouts  11.1 us (5%)
  matrix products  6.95 us (3%)
    psum x1, waiting for transfers between devices, on_device(): lax.psum(partial_value.astype(jnp.bfloat16), 'feat').astype(jnp.float32)  87.6 us
    reduce_scatter x1, waiting for transfers between devices, on_device(): lax.psum_scatter(lax.fori_loop(0, 1 * lax.axis_size('layer'), source_one_...  45.6 us
    all_gather x1, waiting for transfers between devices, on_device(): piece = lax.all_gather(activations, 'layer', axis=0, tiled=True)  27.1 us
    all_gather x1, waiting for transfers between devices, on_device(): lax.all_gather(target, 'feat', axis=2, tiled=True)  23.2 us
    all_gather x1, blocking collectives, on_device(): lax.all_gather(dec_bias, 'feat', axis=1, tiled=True)  12.6 us
    dynamic_update_slice x16, local copies, waits for them, and re-layouts, source_one_source(): return lax.dynamic_update_index_in_dim(carried, value, offset, 0)  6.26 us
    convert_element_type x1, other arithmetic, on_device(): error_rounded = full_error.astype(jnp.bfloat16)  5.17 us
    dot_general x1, matrix products, add_one_source(): jnp.dot(source_rows, weights, preferred_element_type=jnp.float32)  5.05 us
  transfers between devices with their start and end apart: 4, of which 4 were waited for; matrix products, arithmetic and copies ran while one was open for 6% of the time, Pallas kernels for 0%

commit v1 on v0

v1 whole, which is shorter than its diff:
```python
import functools

import jax
import jax.numpy as jnp
from jax import lax
from jax.experimental import pallas as pl
from jax.experimental.pallas import tpu as pltpu
from jax.sharding import PartitionSpec as P

MESH = pl.DeviceIdType.MESH
F32 = jnp.float32
BF16 = jnp.bfloat16


def kernel(
    n_layer, n_feat, n_step, n_block, lag_outer,
    pre_ref, dec_ref, bias_ref, tgt_ref,
    err_ref, grad_ref,
    acts, weights, own, arrived, sent, half_in, error, terms, terms_in, tgt,
    w_sem, t_sem, out_sem,
    act_send, act_recv, p_send, p_recv, h_send, h_recv,
    e_in_send, e_out_send, e_recv, f_send, f_recv, term_send, term_recv,
):
    layer, feat = lax.axis_index("layer"), lax.axis_index("feat")
    tokens, width = pre_ref.shape
    model = weights.shape[1]
    shard = tgt.shape[1]
    half = model // 2
    rows_step, rows_block = tokens // n_step, tokens // n_block
    per_block = n_step // n_block
    tile = 512 if model % 512 == 0 else model
    mid = n_feat // 2
    left = feat < mid
    inward = jnp.where(left, feat + 1, feat - 1)
    outward = jnp.where(left, feat - 1, feat + 1)
    has_outward = jnp.logical_and(feat > 0, feat < n_feat - 1)
    is_mid = jnp.logical_or(feat == mid - 1, feat == mid)
    not_mid = jnp.logical_not(is_mid)

    def layer_cols(index):
        return pl.ds(pl.multiple_of(index * width, width), width)

    near = pl.ds(pl.multiple_of(jnp.where(left, 0, half), half), half)
    far = pl.ds(pl.multiple_of(jnp.where(left, half, 0), half), half)
    own_cols = pl.ds(pl.multiple_of(feat * shard, shard), shard)

    def step_rows(i):
        return pl.ds(pl.multiple_of(i * rows_step, rows_step), rows_step)

    def block_rows(b):
        return pl.ds(pl.multiple_of(b * rows_block, rows_block), rows_block)

    def w_copy(s):
        rows = pl.ds(s * width, width)
        return pltpu.make_async_copy(dec_ref.at[rows, :], weights.at[rows, :], w_sem.at[s])

    for s in range(n_layer):
        w_copy(s).start()
    t_copy = pltpu.make_async_copy(tgt_ref, tgt, t_sem)
    t_copy.start()

    barrier = pltpu.get_barrier_semaphore()
    for t in range(n_layer):
        @pl.when(t != layer)
        def _():
            pl.semaphore_signal(barrier, inc=1, device_id=(t, feat), device_id_type=MESH)
    pl.semaphore_signal(barrier, inc=1, device_id=(layer, inward), device_id_type=MESH)

    @pl.when(has_outward)
    def _():
        pl.semaphore_signal(barrier, inc=1, device_id=(layer, outward), device_id_type=MESH)

    acts[:, layer_cols(layer)] = jnp.maximum(pre_ref[...], jnp.zeros((), BF16))
    for s in range(n_layer):
        @pl.when(s > layer)
        def _():
            acts[:, s * width:(s + 1) * width] = jnp.zeros((tokens, width), BF16)

    pl.semaphore_wait(barrier, n_layer + has_outward.astype(jnp.int32))

    def act_copy(t, b, s):
        rows = block_rows(b)
        view = acts.at[rows, layer_cols(s)]
        return pltpu.make_async_remote_copy(
            src_ref=view, dst_ref=view, send_sem=act_send.at[t, b], recv_sem=act_recv.at[s, b],
            device_id=(t, feat), device_id_type=MESH)

    for b in range(n_block):
        for t in reversed(range(1, n_layer)):
            @pl.when(t > layer)
            def _():
                act_copy(t, b, layer).start()

    for s in range(n_layer):
        w_copy(s).wait()
    t_copy.wait()

    def p_copy(i):
        rows = step_rows(i)
        return pltpu.make_async_remote_copy(
            src_ref=sent.at[rows, :], dst_ref=arrived.at[rows, :],
            send_sem=p_send.at[i], recv_sem=p_recv.at[i],
            device_id=(layer, inward), device_id_type=MESH)

    def h_copy(i):
        rows = step_rows(i)
        return pltpu.make_async_remote_copy(
            src_ref=sent.at[rows, far], dst_ref=half_in.at[rows, :],
            send_sem=h_send.at[i], recv_sem=h_recv.at[i],
            device_id=(layer, inward), device_id_type=MESH)

    def e_copy(i, cols, send, recv, to):
        rows = step_rows(i)
        view = error.at[rows, cols]
        return pltpu.make_async_remote_copy(
            src_ref=view, dst_ref=view, send_sem=send.at[i], recv_sem=recv.at[i],
            device_id=(layer, to), device_id_type=MESH)

    def out_copy(i):
        rows = step_rows(i)
        return pltpu.make_async_copy(error.at[rows, own_cols], err_ref.at[rows, :], out_sem.at[i])

    def forward(b):
        rows = block_rows(b)
        for s in range(n_layer - 1):
            @pl.when(s < layer)
            def _():
                act_copy(layer, b, s).wait_recv()

        def one(c, _):
            cols = pl.ds(pl.multiple_of(c * tile, tile), tile)
            own[rows, cols] = jnp.dot(acts[rows, :], weights[:, cols], preferred_element_type=F32)
            return 0

        lax.fori_loop(0, model // tile, one, 0)
        own[rows, own_cols] += bias_ref[...].astype(F32) - tgt[rows, :].astype(F32)

    def send_partial(i):
        rows = step_rows(i)

        @pl.when(has_outward)
        def _():
            p_copy(i).wait_recv()

            @pl.when(is_mid)
            def _():
                sent[rows, far] = (own[rows, far] + arrived[rows, far].astype(F32)).astype(BF16)
                h_copy(i).start()
                own[rows, near] += arrived[rows, near].astype(F32)

            @pl.when(not_mid)
            def _():
                sent[rows, :] = (own[rows, :] + arrived[rows, :].astype(F32)).astype(BF16)
                p_copy(i).start()

        @pl.when(jnp.logical_not(has_outward))
        def _():
            @pl.when(is_mid)
            def _():
                sent[rows, far] = own[rows, far].astype(BF16)
                h_copy(i).start()

            @pl.when(not_mid)
            def _():
                sent[rows, :] = own[rows, :].astype(BF16)
                p_copy(i).start()

    def finish_half(i):
        rows = step_rows(i)
        h_copy(i).wait_recv()
        error[rows, near] = (own[rows, near] + half_in[rows, :].astype(F32)).astype(BF16)
        e_copy(i, near, e_in_send, f_recv, inward).start()

        @pl.when(has_outward)
        def _():
            e_copy(i, near, e_out_send, e_recv, outward).start()

    def pass_error(i):
        @pl.when(not_mid)
        def _():
            e_copy(i, near, e_out_send, e_recv, inward).wait_recv()

            @pl.when(has_outward)
            def _():
                e_copy(i, near, e_out_send, e_recv, outward).start()

        e_copy(i, far, f_send, f_recv, inward).wait_recv()

        @pl.when(has_outward)
        def _():
            e_copy(i, far, f_send, f_recv, outward).start()

        out_copy(i).start()

    def term_copy(s, b, t):
        rows = block_rows(b)
        return pltpu.make_async_remote_copy(
            src_ref=terms.at[rows, layer_cols(s)], dst_ref=terms_in.at[t, rows, :],
            send_sem=term_send.at[s, b], recv_sem=term_recv.at[t, b],
            device_id=(s, feat), device_id_type=MESH)

    def backward(b):
        rows = block_rows(b)
        step = 2 * width

        def one(c, _):
            cols = pl.ds(pl.multiple_of(c * step, step), step)
            terms[rows, cols] = lax.dot_general(
                error[rows, :], weights[cols, :], (((1,), (1,)), ((), ())),
                preferred_element_type=F32).astype(BF16)
            return 0

        lax.fori_loop(0, n_layer // 2, one, 0)
        for s in range(n_layer - 1):
            @pl.when(s < layer)
            def _():
                term_copy(s, b, layer).start()

    def collect(b):
        rows = block_rows(b)
        grad_ref[rows, :] = terms[rows, layer_cols(layer)].astype(F32)
        for t in range(1, n_layer):
            @pl.when(t > layer)
            def _():
                term_copy(layer, b, t).wait_recv()
                grad_ref[rows, :] += terms_in[t, rows, :].astype(F32)

    lag = jnp.where(is_mid, 2, lag_outer)

    def body(i, _):
        @pl.when(jnp.logical_and(i < n_step, lax.rem(i, per_block) == 0))
        def _():
            forward(lax.div(i, per_block))

        @pl.when(i < n_step)
        def _():
            send_partial(i)

        @pl.when(jnp.logical_and(is_mid, jnp.logical_and(i >= 1, i <= n_step)))
        def _():
            finish_half(i - 1)

        j = i - lag

        @pl.when(jnp.logical_and(j >= 0, j < n_step))
        def _():
            pass_error(j)

        @pl.when(jnp.logical_and(j >= 0, jnp.logical_and(j < n_step, lax.rem(j, per_block) == per_block - 1)))
        def _():
            backward(lax.div(j, per_block))

        return 0

    lax.fori_loop(0, n_step + lag_outer, body, 0)

    def tail(b, _):
        collect(b)
        return 0

    lax.fori_loop(0, n_block, tail, 0)

    def drain(i, _):
        @pl.when(not_mid)
        def _():
            p_copy(i).wait_send()

        @pl.when(is_mid)
        def _():
            h_copy(i).wait_send()
            e_copy(i, near, e_in_send, f_recv, inward).wait_send()

        @pl.when(has_outward)
        def _():
            e_copy(i, near, e_out_send, e_recv, outward).wait_send()
            e_copy(i, far, f_send, f_recv, outward).wait_send()

        out_copy(i).wait()
        return 0

    lax.fori_loop(0, n_step, drain, 0)

    def drain_block(b, _):
        for t in range(1, n_layer):
            @pl.when(t > layer)
            def _():
                act_copy(t, b, layer).wait_send()
        for s in range(n_layer - 1):
            @pl.when(s < layer)
            def _():
                term_copy(s, b, layer).wait_send()
        return 0

    lax.fori_loop(0, n_block, drain_block, 0)


def on_device(n_layer, n_feat, pre_acts, decoder, dec_bias, target):
    _, tokens, width = pre_acts.shape
    model = decoder.shape[3]
    shard = target.shape[2]
    n_step, n_block = 16, 4
    any_space = pl.BlockSpec(memory_space=pl.ANY)
    vmem = pl.BlockSpec(memory_space=pltpu.VMEM)
    dma = pltpu.SemaphoreType.DMA
    flops = 4 * tokens * n_layer * width * model
    error, grad = pl.pallas_call(
        functools.partial(kernel, n_layer, n_feat, n_step, n_block, 6),
        out_shape=(
            jax.ShapeDtypeStruct((tokens, shard), BF16),
            jax.ShapeDtypeStruct((tokens, width), F32),
        ),
        in_specs=[vmem, any_space, vmem, any_space],
        out_specs=(any_space, vmem),
        scratch_shapes=[
            pltpu.VMEM((tokens, n_layer * width), BF16),
            pltpu.VMEM((n_layer * width, model), BF16),
            pltpu.VMEM((tokens, model), F32),
            pltpu.VMEM((tokens, model), BF16),
            pltpu.VMEM((tokens, model), BF16),
            pltpu.VMEM((tokens, model // 2), BF16),
            pltpu.VMEM((tokens, model), BF16),
            pltpu.VMEM((tokens, n_layer * width), BF16),
            pltpu.VMEM((n_layer, tokens, width), BF16),
            pltpu.VMEM((tokens, shard), BF16),
            dma((n_layer,)), dma, dma((n_step,)),
            dma((n_layer, n_block)), dma((n_layer, n_block)),
            dma((n_step,)), dma((n_step,)), dma((n_step,)), dma((n_step,)),
            dma((n_step,)), dma((n_step,)), dma((n_step,)), dma((n_step,)), dma((n_step,)),
            dma((n_layer, n_block)), dma((n_layer, n_block)),
        ],
        compiler_params=pltpu.CompilerParams(
            collective_id=0, has_side_effects=True, vmem_limit_bytes=50 * 1024 * 1024),
        cost_estimate=pl.CostEstimate(
            flops=flops, bytes_accessed=2 * n_layer * width * model, transcendentals=0),
    )(
        pre_acts[0],
        decoder.reshape(n_layer * width, model),
        dec_bias,
        target[0],
    )
    recon_error = error.astype(F32)[None]
    pre_grad = jnp.where(pre_acts > 0, grad[None], 0.0)
    return recon_error, pre_grad


def solution(mesh):
    return jax.shard_map(
        functools.partial(on_device, mesh.shape["layer"], mesh.shape["feat"]),
        mesh=mesh,
        in_specs=(
            P("layer", None, "feat"),
            P("layer", None, "feat", None),
            P("layer", "feat"),
            P("layer", None, "feat"),
        ),
        out_specs=(P("layer", None, "feat"), P("layer", None, "feat")),
        check_vma=False,
    )
```

time: 242 us -> 88 us (0.36)
  waiting for transfers between devices: 184 us -> 0 us
  Pallas kernels: 0 us -> 82.7 us
  between operations: 13.8 us -> 0.65 us
  blocking collectives: 12.6 us -> 0 us
  other arithmetic: 12.5 us -> 1.83 us
  local copies, waits for them, and re-layouts: 11.1 us -> 2.62 us
  matrix products: 6.95 us -> 0 us
    psum x1 -> x0, waiting for transfers between devices: 87.6 us -> none  [on_device(): lax.psum(partial_value.astype(jnp.bfloat16), 'feat').astype(jnp.float32)]
    pallas_call x0 -> x1, Pallas kernels: none -> 82.7 us  [on_device(): pl.pallas_call(functools.partial(kernel, n_layer, n_feat, n_step, n_block...]
    all_gather x2 -> x0, waiting for transfers between devices: 50.3 us -> none  [the longest x1 27.1 us: on_device(): piece = lax.all_gather(activations, 'layer', axis=0, tiled=True)]
    reduce_scatter x1 -> x0, waiting for transfers between devices: 45.6 us -> none  [on_device(): lax.psum_scatter(lax.fori_loop(0, 1 * lax.axis_size('layer'), source_one_...]
    all_gather x1 -> x0, blocking collectives: 12.6 us -> none  [on_device(): lax.all_gather(dec_bias, 'feat', axis=1, tiled=True)]
    convert_element_type x2 -> x0, other arithmetic: 9.31 us -> none  [the longest x1 5.17 us: on_device(): error_rounded = full_error.astype(jnp.bfloat16)]
    dot_general x2 -> x0, matrix products: 6.95 us -> none  [the longest x1 5.05 us: add_one_source(): jnp.dot(source_rows, weights, preferred_element_type=jnp.float32)]
    dynamic_update_slice x16 -> x0, local copies, waits for them, and re-layouts: 6.26 us -> none  [source_one_source(): return lax.dynamic_update_index_in_dim(carried, value, offset, 0)]
  transfers between devices with their start and end apart: 4 -> 0, of which waited for: 4 -> 0; matrix products, arithmetic and copies ran while one was open for 6% -> 0% of each run, Pallas kernels for 0% -> 0%
where the time goes in v1:
time: 88 us; the launch traced here: 87.8 us
  Pallas kernels  82.7 us (94%)
  local copies, waits for them, and re-layouts  2.62 us (3%)
  other arithmetic  1.83 us (2%)
    pallas_call x1, Pallas kernels, on_device(): pl.pallas_call(functools.partial(kernel, n_layer, n_feat, n_step, n_block...  82.7 us
    unnamed x6, local copies, waits for them, and re-layouts  2.62 us

profile of v1, /device:TPU:0, one launch (start us, length us, event | category | flops | bytes accessed | tf_op | source)
XLA Modules:
  0.0 87.8 jit_solution(15358114026990253361)
XLA Ops:
  0.6 0.0 copy-start
  0.6 0.9 %copy-done = bf16[1,512,128]{2,1,0:T(8,128)(2,1)S(1)} copy-done((bf16[1,512,128]{2,1,0:T(8,128)(2,1)S(1)}, bf16[1,512,128]{2,1,0:T(8,128)(2,1)}, u32[]{:S(2)}) %copy-start) | copy-done | bytes 131096
  1.5 0.0 copy-start.1
  1.5 1.0 %copy-done.1 = bf16[1,512,512]{2,1,0:T(8,128)(2,1)S(1)} copy-done((bf16[1,512,512]{2,1,0:T(8,128)(2,1)S(1)}, bf16[1,512,512]{2,1,0:T(8,128)(2,1)}, u32[]{:S(2)}) %copy-start.1) | copy-done | bytes 524312
  2.6 0.0 copy-start.2
  2.6 0.7 copy-done.2
  3.3 82.7 %shard_map.59 = (bf16[512,512]{1,0:T(8,128)(2,1)S(1)}, f32[512,128]{1,0:T(8,128)S(1)}) custom-call(bf16[512,128]{1,0:T(8,128)(2,1)S(1)} %bitcast.8, bf16[1024,2048]{1,0:T(8,128)(2,1)} %bitcast.10, bf16[1,512]{1,0:T(2,128)(2,1)S(1)} %copy-done.2, bf16[512,512]{1,0:T(8,128)(2,1)S(1)} %bitcast.9), custom_call_target="tpu_custom_call" | custom-call | flops 4294967296 | bytes 4194304 | tf_op jit(solution)/shard_map/pallas_call | solution.py:306
  86.0 0.7 bitcast_select_fusion
  86.7 1.1 %bitcast_convert_fusion = f32[1,512,512]{2,1,0:T(8,128)} fusion(bf16[512,512]{1,0:T(8,128)(2,1)S(1)} %get-tuple-element.4), kind=kLoop, calls=%fused_computation | loop fusion | flops 262144 | bytes 1572864 | tf_op jit(solution)/shard_map/broadcast_in_dim | solution.py:341
Async XLA Ops:
  0.6 0.9 %copy-start = (bf16[1,512,128]{2,1,0:T(8,128)(2,1)S(1)}, bf16[1,512,128]{2,1,0:T(8,128)(2,1)}, u32[]{:S(2)}) copy-start(bf16[1,512,128]{2,1,0:T(8,128)(2,1)} %param.4) | copy-start | bytes 393220
  1.5 1.0 %copy-start.1 = (bf16[1,512,512]{2,1,0:T(8,128)(2,1)S(1)}, bf16[1,512,512]{2,1,0:T(8,128)(2,1)}, u32[]{:S(2)}) copy-start(bf16[1,512,512]{2,1,0:T(8,128)(2,1)} %param.7) | copy-start | bytes 1572868
  2.6 0.7 copy-start.2

commit v2 on v1

--- a/solution.py
+++ b/solution.py
@@ -13,16 +13,16 @@
 
 
 def kernel(
-    n_layer, n_feat, n_step, n_block, lag_outer,
+    n_layer, n_feat, n_step, n_block, lag_half, lag_mid, lag_outer,
     pre_ref, dec_ref, bias_ref, tgt_ref,
     err_ref, grad_ref,
-    acts, weights, own, arrived, sent, half_in, error, terms, terms_in, tgt,
-    w_sem, t_sem, out_sem,
+    acts, weights, own, arrived, sent, half_in, error, terms, terms_in, tgt, pre, bias,
+    w_sem, t_sem, pre_sem, bias_sem, out_sem,
     act_send, act_recv, p_send, p_recv, h_send, h_recv,
     e_in_send, e_out_send, e_recv, f_send, f_recv, term_send, term_recv,
 ):
     layer, feat = lax.axis_index("layer"), lax.axis_index("feat")
-    tokens, width = pre_ref.shape
+    tokens, width = pre.shape
     model = weights.shape[1]
     shard = tgt.shape[1]
     half = model // 2
@@ -50,6 +50,11 @@
     def block_rows(b):
         return pl.ds(pl.multiple_of(b * rows_block, rows_block), rows_block)
 
+    pre_copy = pltpu.make_async_copy(pre_ref, pre, pre_sem)
+    pre_copy.start()
+    bias_copy = pltpu.make_async_copy(bias_ref, bias, bias_sem)
+    bias_copy.start()
+
     def w_copy(s):
         rows = pl.ds(s * width, width)
         return pltpu.make_async_copy(dec_ref.at[rows, :], weights.at[rows, :], w_sem.at[s])
@@ -70,7 +75,8 @@
     def _():
         pl.semaphore_signal(barrier, inc=1, device_id=(layer, outward), device_id_type=MESH)
 
-    acts[:, layer_cols(layer)] = jnp.maximum(pre_ref[...], jnp.zeros((), BF16))
+    pre_copy.wait()
+    acts[:, layer_cols(layer)] = jnp.maximum(pre[...], jnp.zeros((), BF16))
     for s in range(n_layer):
         @pl.when(s > layer)
         def _():
@@ -85,15 +91,14 @@
             src_ref=view, dst_ref=view, send_sem=act_send.at[t, b], recv_sem=act_recv.at[s, b],
             device_id=(t, feat), device_id_type=MESH)
 
-    for b in range(n_block):
+    def send_acts(b):
         for t in reversed(range(1, n_layer)):
             @pl.when(t > layer)
             def _():
                 act_copy(t, b, layer).start()
 
-    for s in range(n_layer):
-        w_copy(s).wait()
-    t_copy.wait()
+    send_acts(0)
+
 
     def p_copy(i):
         rows = step_rows(i)
@@ -133,7 +138,7 @@
             return 0
 
         lax.fori_loop(0, model // tile, one, 0)
-        own[rows, own_cols] += bias_ref[...].astype(F32) - tgt[rows, :].astype(F32)
+        own[rows, own_cols] += bias[...].astype(F32) - tgt[rows, :].astype(F32)
 
     def send_partial(i):
         rows = step_rows(i)
@@ -225,20 +230,26 @@
                 term_copy(layer, b, t).wait_recv()
                 grad_ref[rows, :] += terms_in[t, rows, :].astype(F32)
 
-    lag = jnp.where(is_mid, 2, lag_outer)
+    lag = jnp.where(is_mid, lag_mid, lag_outer)
+
+    for s in range(n_layer):
+        w_copy(s).wait()
+    t_copy.wait()
+    bias_copy.wait()
+    forward(0)
+    if n_block > 1:
+        send_acts(1)
 
     def body(i, _):
-        @pl.when(jnp.logical_and(i < n_step, lax.rem(i, per_block) == 0))
-        def _():
-            forward(lax.div(i, per_block))
+        h = i - lag_half
 
         @pl.when(i < n_step)
         def _():
             send_partial(i)
 
-        @pl.when(jnp.logical_and(is_mid, jnp.logical_and(i >= 1, i <= n_step)))
-        def _():
-            finish_half(i - 1)
+        @pl.when(jnp.logical_and(is_mid, jnp.logical_and(h >= 0, h < n_step)))
+        def _():
+            finish_half(h)
 
         j = i - lag
 
@@ -248,17 +259,32 @@
 
         @pl.when(jnp.logical_and(j >= 0, jnp.logical_and(j < n_step, lax.rem(j, per_block) == per_block - 1)))
         def _():
-            backward(lax.div(j, per_block))
+            b = lax.div(j, per_block)
+            backward(b)
+
+            @pl.when(b >= 2)
+            def _():
+                collect(b - 2)
+
+        nxt = lax.div(i + 1, per_block)
+
+        @pl.when(jnp.logical_and(nxt < n_block, lax.rem(i + 1, per_block) == 0))
+        def _():
+            forward(nxt)
+
+            @pl.when(nxt + 1 < n_block)
+            def _():
+                send_acts(nxt + 1)
 
         return 0
 
-    lax.fori_loop(0, n_step + lag_outer, body, 0)
+    lax.fori_loop(0, n_step + max(lag_mid, lag_outer), body, 0)
 
     def tail(b, _):
         collect(b)
         return 0
 
-    lax.fori_loop(0, n_block, tail, 0)
+    lax.fori_loop(max(n_block - 2, 0), n_block, tail, 0)
 
     def drain(i, _):
         @pl.when(not_mid)
@@ -298,18 +324,18 @@
     _, tokens, width = pre_acts.shape
     model = decoder.shape[3]
     shard = target.shape[2]
-    n_step, n_block = 16, 4
+    n_step, n_block = 16, 8
     any_space = pl.BlockSpec(memory_space=pl.ANY)
     vmem = pl.BlockSpec(memory_space=pltpu.VMEM)
     dma = pltpu.SemaphoreType.DMA
     flops = 4 * tokens * n_layer * width * model
     error, grad = pl.pallas_call(
-        functools.partial(kernel, n_layer, n_feat, n_step, n_block, 6),
+        functools.partial(kernel, n_layer, n_feat, n_step, n_block, 1, 3, 8),
         out_shape=(
             jax.ShapeDtypeStruct((tokens, shard), BF16),
             jax.ShapeDtypeStruct((tokens, width), F32),
         ),
-        in_specs=[vmem, any_space, vmem, any_space],
+        in_specs=[any_space] * 4,
         out_specs=(any_space, vmem),
         scratch_shapes=[
             pltpu.VMEM((tokens, n_layer * width), BF16),
@@ -322,14 +348,16 @@
             pltpu.VMEM((tokens, n_layer * width), BF16),
             pltpu.VMEM((n_layer, tokens, width), BF16),
             pltpu.VMEM((tokens, shard), BF16),
-            dma((n_layer,)), dma, dma((n_step,)),
+            pltpu.VMEM((tokens, width), BF16),
+            pltpu.VMEM((1, shard), BF16),
+            dma((n_layer,)), dma, dma, dma, dma((n_step,)),
             dma((n_layer, n_block)), dma((n_layer, n_block)),
             dma((n_step,)), dma((n_step,)), dma((n_step,)), dma((n_step,)),
             dma((n_step,)), dma((n_step,)), dma((n_step,)), dma((n_step,)), dma((n_step,)),
             dma((n_layer, n_block)), dma((n_layer, n_block)),
         ],
         compiler_params=pltpu.CompilerParams(
-            collective_id=0, has_side_effects=True, vmem_limit_bytes=50 * 1024 * 1024),
+            collective_id=0, has_side_effects=True, vmem_limit_bytes=62 * 1024 * 1024),
         cost_estimate=pl.CostEstimate(
             flops=flops, bytes_accessed=2 * n_layer * width * model, transcendentals=0),
     )(

time: 88 us -> 83.8 us (0.952)
  Pallas kernels: 82.7 us -> 79.1 us
  local copies, waits for them, and re-layouts: 2.62 us -> 0.01 us
  other arithmetic: 1.83 us -> 3.83 us
    pallas_call x1, Pallas kernels: 82.7 us -> 79.1 us  [on_device(): pl.pallas_call(functools.partial(kernel, n_layer, n_feat, n_step, n_block...]
    unnamed x6 -> x2, local copies, waits for them, and re-layouts: 2.62 us -> 0.01 us
    broadcast_in_dim x1, other arithmetic: 1.1 us -> 2.14 us  [on_device(): recon_error = error.astype(F32)[None]]
    select_n x1, other arithmetic: 0.73 us -> 1.68 us  [on_device(): pre_grad = jnp.where(pre_acts > 0, grad[None], 0.0)]
where the time goes in v2:
time: 83.8 us; the launch traced here: 83.6 us
  Pallas kernels  79.1 us (94%)
  other arithmetic  3.83 us (5%)
    pallas_call x1, Pallas kernels, on_device(): pl.pallas_call(functools.partial(kernel, n_layer, n_feat, n_step, n_block...  79.1 us
    broadcast_in_dim x1, other arithmetic, on_device(): recon_error = error.astype(F32)[None]  2.14 us
    select_n x1, other arithmetic, on_device(): pre_grad = jnp.where(pre_acts > 0, grad[None], 0.0)  1.68 us

profile of v2, /device:TPU:0, one launch (start us, length us, event | category | flops | bytes accessed | tf_op | source)
XLA Modules:
  0.0 83.6 jit_solution(18237549433884691137)
XLA Ops:
  0.6 0.0 copy-start
  0.6 79.1 %shard_map.59 = (bf16[512,512]{1,0:T(8,128)(2,1)}, f32[512,128]{1,0:T(8,128)}) custom-call(bf16[512,128]{1,0:T(8,128)(2,1)} %bitcast.8, bf16[1024,2048]{1,0:T(8,128)(2,1)} %bitcast.9, bf16[1,512]{1,0:T(2,128)(2,1)} %bias_ref.1, bf16[512,512]{1,0:T(8,128)(2,1)} %bitcast.10), custom_call_target="tpu_custom_call" | custom-call | flops 4294967296 | bytes 4194304 | tf_op jit(solution)/shard_map/pallas_call | solution.py:332
  79.8 0.0 copy-done
  79.8 1.7 %bitcast_select_fusion = f32[1,512,128]{2,1,0:T(8,128)} fusion(f32[512,128]{1,0:T(8,128)} %get-tuple-element.5, bf16[1,512,128]{2,1,0:T(8,128)(2,1)S(1)} %copy-done), kind=kLoop, calls=%fused_computation.1 | loop fusion | flops 131072 | bytes 655360 | tf_op jit(solution)/shard_map/jit(_where)/select_n | solution.py:370
  81.4 2.1 %bitcast_convert_fusion = f32[1,512,512]{2,1,0:T(8,128)} fusion(bf16[512,512]{1,0:T(8,128)(2,1)} %get-tuple-element.4), kind=kLoop, calls=%fused_computation | loop fusion | flops 262144 | bytes 1572864 | tf_op jit(solution)/shard_map/broadcast_in_dim | solution.py:369
Async XLA Ops:
  0.6 79.1 %copy-start = (bf16[1,512,128]{2,1,0:T(8,128)(2,1)S(1)}, bf16[1,512,128]{2,1,0:T(8,128)(2,1)}, u32[]{:S(2)}) copy-start(bf16[1,512,128]{2,1,0:T(8,128)(2,1)} %param.4) | copy-start | bytes 393220

commit v3 on v2

--- a/solution.py
+++ b/solution.py
@@ -28,7 +28,7 @@
     half = model // 2
     rows_step, rows_block = tokens // n_step, tokens // n_block
     per_block = n_step // n_block
-    tile = 512 if model % 512 == 0 else model
+    tile = model // 2
     mid = n_feat // 2
     left = feat < mid
     inward = jnp.where(left, feat + 1, feat - 1)
@@ -206,7 +206,8 @@
 
     def backward(b):
         rows = block_rows(b)
-        step = 2 * width
+        group = 4 if n_layer % 4 == 0 else 1
+        step = group * width
 
         def one(c, _):
             cols = pl.ds(pl.multiple_of(c * step, step), step)
@@ -215,7 +216,7 @@
                 preferred_element_type=F32).astype(BF16)
             return 0
 
-        lax.fori_loop(0, n_layer // 2, one, 0)
+        lax.fori_loop(0, n_layer // group, one, 0)
         for s in range(n_layer - 1):
             @pl.when(s < layer)
             def _():

time: 83.8 us -> 82.8 us (0.988)
  Pallas kernels: 79.1 us -> 78.1 us
    pallas_call x1, Pallas kernels: 79.1 us -> 78.1 us  [on_device(): pl.pallas_call(functools.partial(kernel, n_layer, n_feat, n_step, n_block...]
where the time goes in v3:
time: 82.8 us; the launch traced here: 82.6 us
  Pallas kernels  78.1 us (94%)
  other arithmetic  3.83 us (5%)
    pallas_call x1, Pallas kernels, on_device(): pl.pallas_call(functools.partial(kernel, n_layer, n_feat, n_step, n_block...  78.1 us
    broadcast_in_dim x1, other arithmetic, on_device(): recon_error = error.astype(F32)[None]  2.14 us
    select_n x1, other arithmetic, on_device(): pre_grad = jnp.where(pre_acts > 0, grad[None], 0.0)  1.68 us

profile of v3, /device:TPU:0, one launch (start us, length us, event | category | flops | bytes accessed | tf_op | source)
XLA Modules:
  0.0 82.6 jit_solution(11277566646803162995)
XLA Ops:
  0.6 0.0 copy-start
  0.6 78.1 %shard_map.59 = (bf16[512,512]{1,0:T(8,128)(2,1)}, f32[512,128]{1,0:T(8,128)}) custom-call(bf16[512,128]{1,0:T(8,128)(2,1)} %bitcast.8, bf16[1024,2048]{1,0:T(8,128)(2,1)} %bitcast.9, bf16[1,512]{1,0:T(2,128)(2,1)} %bias_ref.1, bf16[512,512]{1,0:T(8,128)(2,1)} %bitcast.10), custom_call_target="tpu_custom_call" | custom-call | flops 4294967296 | bytes 4194304 | tf_op jit(solution)/shard_map/pallas_call | solution.py:333
  78.8 0.0 copy-done
  78.8 1.7 %bitcast_select_fusion = f32[1,512,128]{2,1,0:T(8,128)} fusion(f32[512,128]{1,0:T(8,128)} %get-tuple-element.5, bf16[1,512,128]{2,1,0:T(8,128)(2,1)S(1)} %copy-done), kind=kLoop, calls=%fused_computation.1 | loop fusion | flops 131072 | bytes 655360 | tf_op jit(solution)/shard_map/jit(_where)/select_n | solution.py:371
  80.5 2.1 %bitcast_convert_fusion = f32[1,512,512]{2,1,0:T(8,128)} fusion(bf16[512,512]{1,0:T(8,128)(2,1)} %get-tuple-element.4), kind=kLoop, calls=%fused_computation | loop fusion | flops 262144 | bytes 1572864 | tf_op jit(solution)/shard_map/broadcast_in_dim | solution.py:370
Async XLA Ops:
  0.6 78.2 %copy-start = (bf16[1,512,128]{2,1,0:T(8,128)(2,1)S(1)}, bf16[1,512,128]{2,1,0:T(8,128)(2,1)}, u32[]{:S(2)}) copy-start(bf16[1,512,128]{2,1,0:T(8,128)(2,1)} %param.4) | copy-start | bytes 393220
